TPU v7x, 32 devices: a whole 2x2x4 slice. The times are simulated.
32 devices in a mesh: groups: 2 (over y), samp: 4 (over z), cent: 4 (over x, core).
Axes of the slice: x: 2, y: 2, z: 4, core: 2. Of those that a mesh axis runs over, the one named last changes fastest.
Arguments:
- samples: bfloat16 [8192, 1024], P(('groups', 'samp')), parts along dimension 0, may hold values from -16 to 16, as said below
- targets: float32 [8192], P(('groups', 'samp')), parts along dimension 0, may hold values from -2 to 4
- centres: bfloat16 [2048, 1024], P(('groups', 'cent')), parts along dimension 0, may hold values from -16 to 16, as said below
- tri_inv: float32 [2048, 1024], P(('groups', 'cent'), 'samp'), parts along dimension 0, as said below
- inner_inv: float32 [2048, 1024], P(('groups', 'cent'), 'samp'), parts along dimension 0, as said below
Outputs:
- fitted: float32 [8192], P(('groups', 'samp')), parts along dimension 0
There are 2 independent parts, one for each index of `groups`. A program takes and returns all parts, laid end to end along the dimension named above; each array names one. Nothing has to cross between parts.
Inputs may be any that keep to these rules, and one draw needn't show every extreme that they name: `samples`: entries are rows of points with varying norms. `centres`: entries are rows of points with varying norms. `tri_inv`: upper triangular with a positive diagonal. `inner_inv`: upper triangular with a positive diagonal.
All inputs are finite; a program needn't handle non-finite values.
Results may differ from a plain program's by a relative error of at most 0.0003.
Values sent between devices are 32-bit elements; how exact they have to be, the bound alone decides.
A program may use at most 64 MiB of HBM per device.

v0:
```python
import jax
import jax.numpy as jnp
from jax import lax
from jax.sharding import PartitionSpec as P

ITERS = 2


ridge_weight = 0.01
exact_mode = lax.Precision.HIGHEST


def body(samples, targets, centres, tri_inv, inner_inv):
    row_count = samples.shape[0]
    feat_width = samples.shape[1]
    cent_count = centres.shape[0]
    block_rows = min(512, row_count)
    turn_count = row_count // block_rows
    total_rows = row_count * lax.axis_size("samp")
    exponent_scale = 1.0 / feat_width
    centre_norms = jnp.einsum("cf,cf->c", centres, centres, preferred_element_type=jnp.float32)
    row_norms = jnp.einsum("rf,rf->r", samples, samples, preferred_element_type=jnp.float32)

    def kernel_tile(sample_block, norm_block):
        crossed = lax.dot_general(
            sample_block, centres, (((1,), (1,)), ((), ())), preferred_element_type=jnp.float32
        )
        return jnp.exp(
            (2.0 * crossed - norm_block[:, None] - centre_norms[None, :]) * exponent_scale
        )

    def block_tile(turn_index):
        start_row = turn_index * block_rows
        sample_block = lax.dynamic_slice_in_dim(samples, start_row, block_rows, 0)
        norm_block = lax.dynamic_slice_in_dim(row_norms, start_row, block_rows, 0)
        return kernel_tile(sample_block, norm_block)

    def apply_rows(vector):

        def advance(turn_index, running):
            products = jnp.dot(block_tile(turn_index), vector, precision=exact_mode)
            return lax.dynamic_update_slice_in_dim(running, products, turn_index * block_rows, 0)

        return lax.fori_loop(0, turn_count, advance, jnp.zeros((row_count,), jnp.float32))

    def apply_cols(vector):

        def advance(turn_index, running):
            weight_block = lax.dynamic_slice_in_dim(vector, turn_index * block_rows, block_rows, 0)
            return running + jnp.dot(weight_block, block_tile(turn_index), precision=exact_mode)

        return lax.fori_loop(0, turn_count, advance, jnp.zeros((cent_count,), jnp.float32))

    def kernel_forward(vector):
        return lax.psum(apply_rows(vector), "cent")

    def kernel_back(vector):
        return lax.psum(apply_cols(vector), "samp")

    tri_matrix, inner_matrix = (
        lax.all_gather(tri_inv, "samp", axis=1, tiled=True),
        lax.all_gather(inner_inv, "samp", axis=1, tiled=True),
    )

    def forward_local(matrix, joined):
        return jnp.dot(matrix, joined, precision=exact_mode)

    def backward(matrix, vector):
        return lax.psum_scatter(
            jnp.dot(vector, matrix, precision=exact_mode), "cent", scatter_dimension=0, tiled=True
        )

    def forward(matrix, vector):
        joined = lax.all_gather(vector, "cent", axis=0, tiled=True)
        return forward_local(matrix, joined)

    rhs = backward(inner_matrix, backward(tri_matrix, kernel_back(targets)) / total_rows)
    solution = jnp.zeros((cent_count,), jnp.float32)
    residual = rhs

    def inner_total(first, second):
        return lax.psum(jnp.sum(first * second), "cent")

    direction = rhs
    norm_now = inner_total(residual, residual)
    for advance_index in range(ITERS):
        lifted = forward(inner_matrix, direction)
        expanded = forward(tri_matrix, lifted)
        row_values = kernel_forward(expanded)
        column_values = kernel_back(row_values)
        combined = backward(tri_matrix, column_values) / total_rows + ridge_weight * lifted
        mapped = backward(inner_matrix, combined)
        step_size = norm_now / inner_total(direction, mapped)
        solution = solution + step_size * direction
        residual = residual - step_size * mapped
        norm_next = inner_total(residual, residual)
        direction = residual + norm_next / norm_now * direction
        norm_now = norm_next
    coefficients = forward(tri_matrix, forward(inner_matrix, solution))
    return kernel_forward(coefficients)


def solution(mesh):
    in_specs = (
        P(("groups", "samp"), None),
        P(("groups", "samp")),
        P(("groups", "cent"), None),
        P(("groups", "cent"), "samp"),
        P(("groups", "cent"), "samp"),
    )
    out_specs = P(("groups", "samp"))
    return jax.shard_map(body, mesh=mesh, in_specs=in_specs, out_specs=out_specs, check_vma=False)
```

profile of v0, /device:TPU:0, one launch (start us, length us, event | category | flops | bytes accessed | tf_op | source)
XLA Modules:
  0.0 236.6 jit_solution(6103582041225097782)
XLA Ops:
  8.1 2.1 fusion.36
  11.6 2.0 while.84
  13.6 13.7 %psum.70 = f32[256]{0:T(256)S(1)} all-reduce(f32[256]{0:T(256)S(1)} %get-tuple-element.749), channel_id=1, replica_groups=mesh['groups'=2,'samp'=4,'cent'=4] {'samp'}, use_global_device_ids=true, to_apply=%region_2.0 | all-reduce | flops 256 | bytes 2048 | tf_op jit(solution)/shard_map/psum | solution.py:58
  27.3 12.3 %all-gather.9.cloned.1.call-done = f32[256,1024]{1,0:T(8,128)} async-done(((f32[256,256]{1,0:T(8,128)}), f32[256,1024]{1,0:T(8,128)}) %all-gather.9.cloned.1.call-update) | async-done | bytes 1048592 | tf_op jit(solution)/shard_map/all_gather | solution.py:61
  39.7 1.9 fusion.47
  41.6 6.4 %all-reduce = f32[1024]{0:T(1024)S(1)} all-reduce(f32[1024]{0:T(1024)S(1)} %bitcast.182), channel_id=2, replica_groups=mesh['groups'=2,'samp'=4,'cent'=4] {'cent'}, use_global_device_ids=true, to_apply=%region_3.0.clone | all-reduce | flops 1024 | bytes 8192
  48.1 20.7 %all-gather.11.cloned.1.call-done = f32[256,1024]{1,0:T(8,128)} async-done(((f32[256,256]{1,0:T(8,128)}), f32[256,1024]{1,0:T(8,128)}) %all-gather.11.cloned.1.call-update) | async-done | bytes 1048592 | tf_op jit(solution)/shard_map/all_gather | solution.py:62
  68.8 1.8 fusion.48
  70.6 6.4 %all-reduce.1 = f32[1024]{0:T(1024)S(1)} all-reduce(f32[1024]{0:T(1024)S(1)} %bitcast.183), channel_id=3, replica_groups=mesh['groups'=2,'samp'=4,'cent'=4] {'cent'}, use_global_device_ids=true, to_apply=%region_4.0.clone | all-reduce | flops 1024 | bytes 8192
  77.1 5.1 %all-gather = f32[4,1,256]{2,1,0:T(1,128)S(1)} all-gather(f32[1,1,256]{2,1,0:T(1,128)S(1)} %bitcast.199), channel_id=1, replica_groups=mesh['groups'=2,'samp'=4,'cent'=4] {'cent'}, dimensions={0}, use_global_device_ids=true | all-gather | bytes 5120 | tf_op jit(solution)/shard_map/all_gather | solution.py:74
  82.2 2.1 fusion.49
  84.3 5.1 %all-gather.1 = f32[4,1,256]{2,1,0:T(1,128)S(1)} all-gather(f32[1,1,256]{2,1,0:T(1,128)S(1)} %bitcast.189), channel_id=1, replica_groups=mesh['groups'=2,'samp'=4,'cent'=4] {'cent'}, dimensions={0}, use_global_device_ids=true | all-gather | bytes 5120 | tf_op jit(solution)/shard_map/all_gather | solution.py:74
  89.4 0.9 fusion.50
  90.3 4.7 %while.81 = (s32[]{:T(128)}, f32[1024]{0:T(1024)S(1)}, bf16[1024,1024]{1,0:T(8,128)(2,1)S(1)}, bf16[256,1024]{1,0:T(8,128)(2,1)}, f32[1024]{0:T(1024)S(1)}, /*in...) while((s32[]{:T(128)}, f32[1024]{0:T(1024)S(1)}, ...), condition=%wide.region_8.0_spmd, body=%wide.region_7.0_spmd.sunk | while | flops 270532608 | bytes 2635943 | solution.py:44
  90.4 1.5 fusion.140
  92.7 1.5 fusion.140
  95.0 6.5 %psum.72 = f32[1024]{0:T(1024)S(1)} all-reduce(f32[1024]{0:T(1024)S(1)} %get-tuple-element.750), channel_id=1, replica_groups=mesh['groups'=2,'samp'=4,'cent'=4] {'cent'}, use_global_device_ids=true, to_apply=%region_9.0 | all-reduce | flops 1024 | bytes 8192 | tf_op jit(solution)/shard_map/psum | solution.py:55
  101.5 4.8 %while.85 = (s32[]{:T(128)}, f32[256]{0:T(256)S(1)}, f32[1024]{0:T(1024)S(1)}, bf16[1024,1024]{1,0:T(8,128)(2,1)}, bf16[256,1024]{1,0:T(8,128)(2,1)}, /*index=5*...) while((s32[]{:T(128)}, f32[256]{0:T(256)S(1)}, ...), condition=%wide.region_11.0_spmd.clone, body=%wide.region_10.0_spmd.clone.sunk | while | flops 270533120 | bytes 2639025 | solution.py:52
  101.6 1.9 fusion.164
  104.1 1.8 fusion.164
  106.3 10.3 %psum.73 = f32[256]{0:T(256)S(1)} all-reduce(f32[256]{0:T(256)S(1)} %get-tuple-element.751), channel_id=1, replica_groups=mesh['groups'=2,'samp'=4,'cent'=4] {'samp'}, use_global_device_ids=true, to_apply=%region_12.0 | all-reduce | flops 256 | bytes 2048 | tf_op jit(solution)/shard_map/psum | solution.py:58
  117.2 5.6 %all-reduce.2 = f32[1024]{0:T(1024)S(1)} all-reduce(f32[1024]{0:T(1024)S(1)} %bitcast.184), channel_id=4, replica_groups=mesh['groups'=2,'samp'=4,'cent'=4] {'cent'}, use_global_device_ids=true, to_apply=%region_13.0.clone | all-reduce | flops 1024 | bytes 8192
  123.6 6.5 %all-reduce.3 = f32[1024]{0:T(1024)S(1)} all-reduce(f32[1024]{0:T(1024)S(1)} %bitcast.185), channel_id=5, replica_groups=mesh['groups'=2,'samp'=4,'cent'=4] {'cent'}, use_global_device_ids=true, to_apply=%region_14.0.clone | all-reduce | flops 1024 | bytes 8192
  130.8 6.6 %all-reduce.6 = (f32[]{:T(128)}, f32[]{:T(128)}) all-reduce(f32[]{:T(128)} %get-tuple-element.828, f32[]{:T(128)} %get-tuple-element.827), channel_id=1, replica_groups=mesh['groups'=2,'samp'=4,'cent'=4] {'cent'}, use_global_device_ids=true, to_apply=%region_6.0 | all-reduce | flops 2 | bytes 16 | tf_op jit(solution)/shard_map/psum | solution.py:82
  139.4 6.7 %psum.75 = f32[]{:T(128)} all-reduce(f32[]{:T(128)} %multiply_reduce_fusion), channel_id=1, replica_groups=mesh['groups'=2,'samp'=4,'cent'=4] {'cent'}, use_global_device_ids=true, to_apply=%region_18.0 | all-reduce | flops 1 | bytes 8 | tf_op jit(solution)/shard_map/psum | solution.py:82
  147.4 5.1 %all-gather.2 = f32[4,1,256]{2,1,0:T(1,128)S(1)} all-gather(f32[1,1,256]{2,1,0:T(1,128)S(1)} %bitcast.188), channel_id=1, replica_groups=mesh['groups'=2,'samp'=4,'cent'=4] {'cent'}, dimensions={0}, use_global_device_ids=true | all-gather | bytes 5120 | tf_op jit(solution)/shard_map/all_gather | solution.py:74
  152.5 0.9 fusion.53
  153.4 5.1 %all-gather.3 = f32[4,1,256]{2,1,0:T(1,128)S(1)} all-gather(f32[1,1,256]{2,1,0:T(1,128)S(1)} %bitcast.191), channel_id=1, replica_groups=mesh['groups'=2,'samp'=4,'cent'=4] {'cent'}, dimensions={0}, use_global_device_ids=true | all-gather | bytes 5120 | tf_op jit(solution)/shard_map/all_gather | solution.py:74
  158.5 0.9 fusion.54
  159.4 5.1 %while.82 = (s32[]{:T(128)}, f32[1024]{0:T(1024)S(1)}, bf16[1024,1024]{1,0:T(8,128)(2,1)}, bf16[256,1024]{1,0:T(8,128)(2,1)S(1)}, f32[1024]{0:T(1024)S(1)}, /*in...) while((s32[]{:T(128)}, f32[1024]{0:T(1024)S(1)}, ...), condition=%wide.region_20.0_spmd, body=%wide.region_19.0_spmd.sunk | while | flops 270532608 | bytes 2635943 | solution.py:44
  159.5 1.7 fusion.146
  162.0 1.7 fusion.146
  164.5 6.4 %psum.76 = f32[1024]{0:T(1024)S(1)} all-reduce(f32[1024]{0:T(1024)S(1)} %get-tuple-element.752), channel_id=1, replica_groups=mesh['groups'=2,'samp'=4,'cent'=4] {'cent'}, use_global_device_ids=true, to_apply=%region_21.0 | all-reduce | flops 1024 | bytes 8192 | tf_op jit(solution)/shard_map/psum | solution.py:55
  170.9 4.5 %while.86 = (s32[]{:T(128)}, f32[256]{0:T(256)S(1)}, f32[1024]{0:T(1024)S(1)}, bf16[1024,1024]{1,0:T(8,128)(2,1)}, bf16[256,1024]{1,0:T(8,128)(2,1)S(1)}, /*inde...) while((s32[]{:T(128)}, f32[256]{0:T(256)S(1)}, ...), condition=%wide.region_23.0_spmd.clone, body=%wide.region_22.0_spmd.clone.sunk | while | flops 270533120 | bytes 2639025 | solution.py:52
  170.9 1.7 fusion.170
  173.2 1.7 fusion.170
  175.3 8.6 %psum.77 = f32[256]{0:T(256)S(1)} all-reduce(f32[256]{0:T(256)S(1)} %get-tuple-element.753), channel_id=1, replica_groups=mesh['groups'=2,'samp'=4,'cent'=4] {'samp'}, use_global_device_ids=true, to_apply=%region_24.0 | all-reduce | flops 256 | bytes 2048 | tf_op jit(solution)/shard_map/psum | solution.py:58
  184.5 5.6 %all-reduce.4 = f32[1024]{0:T(1024)S(1)} all-reduce(f32[1024]{0:T(1024)S(1)} %bitcast.186), channel_id=6, replica_groups=mesh['groups'=2,'samp'=4,'cent'=4] {'cent'}, use_global_device_ids=true, to_apply=%region_25.0.clone | all-reduce | flops 1024 | bytes 8192
  190.9 6.3 %all-reduce.5 = f32[1024]{0:T(1024)S(1)} all-reduce(f32[1024]{0:T(1024)S(1)} %bitcast.187), channel_id=7, replica_groups=mesh['groups'=2,'samp'=4,'cent'=4] {'cent'}, use_global_device_ids=true, to_apply=%region_26.0.clone | all-reduce | flops 1024 | bytes 8192
  197.9 6.3 %psum.78 = f32[]{:T(128)} all-reduce(f32[]{:T(128)} %fusion.38), channel_id=1, replica_groups=mesh['groups'=2,'samp'=4,'cent'=4] {'cent'}, use_global_device_ids=true, to_apply=%region_28.0 | all-reduce | flops 1 | bytes 8 | tf_op jit(solution)/shard_map/psum | solution.py:82
  205.5 5.1 %all-gather.4 = f32[4,1,256]{2,1,0:T(1,128)S(1)} all-gather(f32[1,1,256]{2,1,0:T(1,128)S(1)} %bitcast.200), channel_id=1, replica_groups=mesh['groups'=2,'samp'=4,'cent'=4] {'cent'}, dimensions={0}, use_global_device_ids=true | all-gather | bytes 5120 | tf_op jit(solution)/shard_map/all_gather | solution.py:74
  210.5 0.9 convolution_bitcast_fusion
  211.4 5.1 %all-gather.5 = f32[4,1,256]{2,1,0:T(1,128)S(1)} all-gather(f32[1,1,256]{2,1,0:T(1,128)S(1)} %convolution_bitcast_fusion), channel_id=1, replica_groups=mesh['groups'=2,'samp'=4,'cent'=4] {'cent'}, dimensions={0}, use_global_device_ids=true | all-gather | bytes 5120 | tf_op jit(solution)/shard_map/all_gather | solution.py:74
  216.5 0.9 fusion.57
  217.4 5.1 %while.83 = (s32[]{:T(128)}, f32[1024]{0:T(1024)S(1)}, bf16[1024,1024]{1,0:T(8,128)(2,1)}, bf16[256,1024]{1,0:T(8,128)(2,1)S(1)}, f32[1024]{0:T(1024)S(1)}, /*in...) while((s32[]{:T(128)}, f32[1024]{0:T(1024)S(1)}, ...), condition=%wide.region_30.0_spmd, body=%wide.region_29.0_spmd.sunk | while | flops 270532608 | bytes 2635943 | solution.py:44
  217.5 1.7 fusion.152
  220.1 1.7 fusion.152
  222.5 7.2 %psum.79 = f32[1024]{0:T(1024)} all-reduce(f32[1024]{0:T(1024)S(1)} %get-tuple-element.754), channel_id=1, replica_groups=mesh['groups'=2,'samp'=4,'cent'=4] {'cent'}, use_global_device_ids=true, to_apply=%region_31.0 | all-reduce | flops 1024 | bytes 8192 | tf_op jit(solution)/shard_map/psum | solution.py:55
  (85 shorter events, 16.1 us)
Async XLA Ops:
  6.5 3.8 %copy-start.7 = (u32[32]{0:T(128)S(1)}, u32[32]{0:T(128)}, u32[]{:S(2)}) copy-start(u32[32]{0:T(128)} %constant.257) | copy-start | bytes 388
  6.5 5.1 %copy-start.2 = (bf16[1024,1024]{1,0:T(8,128)(2,1)S(1)}, bf16[1024,1024]{1,0:T(8,128)(2,1)}, u32[]{:S(2)}) copy-start(bf16[1024,1024]{1,0:T(8,128)(2,1)} %param.17) | copy-start | bytes 6291460
  6.5 3.6 %copy-start.4 = (bf16[256,1024]{1,0:T(8,128)(2,1)S(1)}, bf16[256,1024]{1,0:T(8,128)(2,1)}, u32[]{:S(2)}) copy-start(bf16[256,1024]{1,0:T(8,128)(2,1)} %param.19) | copy-start | bytes 1572868
  6.5 5.1 %copy-start.6 = (f32[1024]{0:T(1024)S(1)}, f32[1024]{0:T(1024)}, u32[]{:S(2)}) copy-start(f32[1024]{0:T(1024)} %param.18) | copy-start | bytes 12292
  6.5 33.2 %all-gather.9.cloned.1.call-start = ((), (), s32[]{:S(2)}) async-start(), calls=%async_computation | async-start | bytes 1310720 | tf_op jit(solution)/shard_map/all_gather | solution.py:61
  7.3 61.5 %all-gather.11.cloned.1.call-start = ((), (), s32[]{:S(2)}) async-start(), calls=%async_computation.1 | async-start | bytes 1310720 | tf_op jit(solution)/shard_map/all_gather | solution.py:62
  39.7 49.7 %copy-start = (f32[256,1024]{1,0:T(8,128)S(1)}, f32[256,1024]{1,0:T(8,128)}, u32[]{:S(2)}) copy-start(f32[256,1024]{1,0:T(8,128)} %all-gather.9.cloned.1.call-done) | copy-start | bytes 3145732
  95.0 6.5 %copy-start.3 = (bf16[1024,1024]{1,0:T(8,128)(2,1)}, bf16[1024,1024]{1,0:T(8,128)(2,1)S(1)}, u32[]{:S(2)}) copy-start(bf16[1024,1024]{1,0:T(8,128)(2,1)S(1)} %get-tuple-element.1376) | copy-start | bytes 6291460
  101.5 21.4 %copy-start.1 = (f32[256,1024]{1,0:T(8,128)S(1)}, f32[256,1024]{1,0:T(8,128)}, u32[]{:S(2)}) copy-start(f32[256,1024]{1,0:T(8,128)} %all-gather.11.cloned.1.call-done) | copy-start | bytes 3145732
  116.6 42.8 %copy-start.5 = (bf16[256,1024]{1,0:T(8,128)(2,1)S(1)}, bf16[256,1024]{1,0:T(8,128)(2,1)}, u32[]{:S(2)}) copy-start(bf16[256,1024]{1,0:T(8,128)(2,1)} %get-tuple-element.1387) | copy-start | bytes 1572868
Sparse Core Ops, SparseCore 0:
  8.9 30.7 all-gather.8
  41.3 27.4 all-gather.10
where the time goes:
time: 238 us; the launch traced here: 237 us
  blocking collectives  140 us (59%)
  matrix products  35.8 us (15%)
  waiting for transfers between devices  34.4 us (14%)
  between operations  18 us (8%)
  other arithmetic  5.04 us (2%)
  local copies, waits for them, and re-layouts  3.35 us (1%)
    unnamed x6, blocking collectives  36.9 us
    psum x3, blocking collectives, kernel_back(): return lax.psum(apply_cols(vector), 'samp')  32.6 us
    all_gather x6, blocking collectives, forward(): joined = lax.all_gather(vector, 'cent', axis=0, tiled=True)  30.4 us
    all_gather x1, waiting for transfers between devices, body(): lax.all_gather(inner_inv, 'samp', axis=1, tiled=True)  20.7 us
    psum x3, blocking collectives, kernel_forward(): return lax.psum(apply_rows(vector), 'cent')  20.1 us
    psum x3, blocking collectives, inner_total(): return lax.psum(jnp.sum(first * second), 'cent')  19.5 us
    dot_general x12, matrix products, kernel_tile(): lax.dot_general(sample_block, centres, (((1,), (1,)), ((), ())), preferre...  18.1 us
    all_gather x1, waiting for transfers between devices, body(): lax.all_gather(tri_inv, 'samp', axis=1, tiled=True)  12.3 us
  transfers between devices with their start and end apart: 2, of which 2 were waited for; matrix products, arithmetic and copies ran while one was open for 3% of the time, Pallas kernels for 0%

commit v1 on v0

v1 whole, which is shorter than its diff:
```python
import functools
import jax
import jax.numpy as jnp
from jax import lax
from jax.experimental import pallas as pl
from jax.experimental.pallas import tpu as pltpu
from jax.sharding import PartitionSpec as P

ITERS = 2
ridge_weight = 0.01
MESH = pl.DeviceIdType.MESH
LANES = 128


def row_to_col(row):
    width = row.shape[1]
    r = lax.broadcasted_iota(jnp.int32, (width, width), 0)
    c = lax.broadcasted_iota(jnp.int32, (width, width), 1)
    return jnp.sum(jnp.where(r == c, row, 0.0), axis=1, keepdims=True)


def col_to_row(col):
    width = col.shape[0]
    r = lax.broadcasted_iota(jnp.int32, (width, width), 0)
    c = lax.broadcasted_iota(jnp.int32, (width, width), 1)
    return jnp.sum(jnp.where(r == c, col, 0.0), axis=0, keepdims=True)


def kernel(n_s, n_c, split, samples_hbm, targets, centres, tri, inner, fitted,
           samples, ktile, tri_row, inner_t, joined,
           col_buf, rhs_buf, vec_buf, row_buf, all_buf,
           load_sem, tri_sem, chain_send, chain_recv, send_sem, recv_sem):
    g = lax.axis_index("groups")
    s = lax.axis_index("samp")
    c = lax.axis_index("cent")
    n = n_s * n_c
    me = s * n_c + c
    cb, feat = centres.shape
    rb = samples_hbm.shape[0]
    sb = inner_t.shape[0]
    total = tri_row.shape[1]
    part = sb // n_c
    total_rows = float(rb * n_s)
    chunk = min(256, rb)
    chunks = rb // chunk

    def at(ss, cc):
        return {"groups": g, "samp": ss, "cent": cc}

    def each(count, act):
        if count <= 16:
            for i in range(1, count):
                act(i)
        else:
            lax.fori_loop(1, count, lambda i, z: (act(i), z)[1], 0)

    def peers(kind, act):
        if kind == "samp":
            each(n_s, lambda i: act(lax.rem(s + i, n_s), c))
        elif kind == "cent":
            each(n_c, lambda i: act(s, lax.rem(c + i, n_c)))
        else:
            each(n, lambda i: act(lax.rem(s + i // n_c, n_s), lax.rem(c + i % n_c, n_c)))

    def loads(j):
        rows = pl.ds(j * chunk, chunk)
        return pltpu.make_async_copy(samples_hbm.at[rows], samples.at[rows], load_sem.at[j])

    barrier = pltpu.get_barrier_semaphore()
    peers("all", lambda a, b: pl.semaphore_signal(barrier, inc=1, device_id=at(a, b), device_id_type=MESH))
    for j in range(chunks):
        loads(j).start()

    def live(k):
        return (k + 1) * sb > c * cb

    def tri_block(k):
        return tri_row.at[:, pl.ds(pl.multiple_of(k * sb, LANES), sb)]

    def inner_slot(k):
        return joined.at[:, pl.ds(pl.multiple_of(k * cb, LANES), cb)]

    if split:
        own_tri = pltpu.make_async_copy(tri, tri_block(s), tri_sem.at[0])
        own_tri.start()
        inner_t[...] = inner[...].T
        for k in range(n_s):
            @pl.when(jnp.logical_not(live(k)) & (k != s))
            def _():
                tri_row[:, k * sb:(k + 1) * sb] = jnp.zeros((cb, sb), jnp.float32)
    else:
        own_tri = pltpu.make_async_copy(tri, tri_row, tri_sem.at[0])
        own_tri.start()
        inner_t[...] = inner[...]

    centre_vals = centres[...]
    wide = centre_vals.astype(jnp.float32)
    centre_norms = jnp.sum(wide * wide, axis=1, keepdims=True)

    def tile(j):
        loads(j).wait()
        block = samples[j * chunk:(j + 1) * chunk, :]
        wide_block = block.astype(jnp.float32)
        norms = col_to_row(jnp.sum(wide_block * wide_block, axis=1, keepdims=True))
        crossed = lax.dot_general(centre_vals, block, (((1,), (1,)), ((), ())),
                                  preferred_element_type=jnp.float32)
        ktile[:, j * chunk:(j + 1) * chunk] = jnp.exp((2.0 * crossed - norms - centre_norms) * (1.0 / feat))

    def hop(way, j):
        k = s - way * j
        lane = (1 - way) // 2
        return pltpu.make_async_remote_copy(
            src_ref=tri_block(k), dst_ref=tri_block(k),
            send_sem=chain_send.at[lane, j], recv_sem=chain_recv.at[lane, j],
            device_id=at(s + way, c), device_id_type=MESH)

    def inside(k):
        return (k >= 0) & (k < n_s)

    def chain_start(j):
        for way in (1, -1):
            k = s - way * j

            @pl.when(inside(k) & inside(s + way) & live(k))
            def _():
                hop(way, j).start()

    def chain_wait(j):
        for way in (1, -1):
            k = s - way * j
            lane = (1 - way) // 2

            @pl.when(inside(k) & live(k))
            def _():
                pltpu.make_async_copy(tri_block(k), tri_block(k), chain_recv.at[lane, j - 1]).wait()

    def chain_finish():
        for j in range(n_s - 1):
            for way in (1, -1):
                k = s - way * j

                @pl.when(inside(k) & inside(s + way) & live(k))
                def _():
                    hop(way, j).wait_send()

    def publish(buf, slot, index, kind):
        peers(kind, lambda a, b: pltpu.make_async_remote_copy(
            src_ref=buf.at[slot], dst_ref=buf.at[slot],
            send_sem=send_sem.at[index], recv_sem=recv_sem.at[index],
            device_id=at(a, b), device_id_type=MESH).start())

    def arrive(buf, index):
        rest = buf.at[pl.ds(0, buf.shape[0] - 1)]
        pltpu.make_async_copy(rest, rest, recv_sem.at[index]).wait()

    def settle(buf, index):
        rest = buf.at[pl.ds(0, buf.shape[0] - 1)]
        pltpu.make_async_copy(rest, rest, send_sem.at[index]).wait()

    def summed(buf, first=0, count=None):
        count = buf.shape[0] if count is None else count
        if count <= 32:
            acc = buf[first]
            for i in range(1, count):
                acc = acc + buf[first + i]
            return acc
        return lax.fori_loop(1, count, lambda i, acc: acc + buf[first + i], buf[first])

    def tail(value):
        return jnp.broadcast_to(value, (1, LANES))

    def square(vector):
        return jnp.sum(vector * vector, axis=1, keepdims=True)

    half = chunks // 2
    for j in range(half):
        tile(j)
    pl.semaphore_wait(barrier, n - 1)
    own_tri.wait()
    if split:
        chain_start(0)

    def inner_copy(i):
        other = lax.rem(c + i, n_c)
        return pltpu.make_async_remote_copy(
            src_ref=inner_t.at[pl.ds(pl.multiple_of(other * part, 8), part)], dst_ref=inner_slot(c),
            send_sem=tri_sem.at[1], recv_sem=tri_sem.at[2],
            device_id=at(s, other), device_id_type=MESH)

    for i in range(1, n_c):
        inner_copy(i).start()
    own_inner = pltpu.make_async_copy(
        inner_t.at[pl.ds(pl.multiple_of(c * part, 8), part)], inner_slot(c), tri_sem.at[3])
    own_inner.start()
    for j in range(half, chunks):
        tile(j)

    aimed = jnp.sum(ktile[...] * targets[...], axis=1, keepdims=True)
    if split:
        col_buf[s] = col_to_row(aimed)
        publish(col_buf, s, 0, "samp")
        if n_s > 1:
            chain_wait(1)
            if n_s > 2:
                chain_start(1)
        arrive(col_buf, 0)
        pulled = row_to_col(summed(col_buf))
        own_block = tri_row[:, pl.ds(pl.multiple_of(s * sb, LANES), sb)]
        rhs_buf[me] = jnp.sum(own_block * pulled, axis=0, keepdims=True)
        publish(rhs_buf, me, 1, "all")
        for j in range(2, n_s):
            chain_wait(j)
            if j < n_s - 1:
                chain_start(j)
        arrive(rhs_buf, 1)
        rh = jnp.concatenate([summed(rhs_buf, k * n_c, n_c) for k in range(n_s)], axis=1)
    else:
        rhs_buf[me] = jnp.sum(tri_row[...] * aimed, axis=0, keepdims=True)
        publish(rhs_buf, me, 1, "all")
        arrive(rhs_buf, 1)
        rh = summed(rhs_buf)
    rh = rh / total_rows

    moved = inner_t.at[pl.ds(0, (n_c - 1) * part)]
    pltpu.make_async_copy(moved, moved, tri_sem.at[2]).wait()
    own_inner.wait()

    def condition(vector, buf, index):
        picked = jnp.sum(joined[...] * vector, axis=1, keepdims=True)
        buf[me, :, :total] = jnp.sum(joined[...] * picked, axis=0, keepdims=True)
        buf[me, :, total:] = tail(jnp.sum(picked * picked, axis=0, keepdims=True))
        publish(buf, me, index, "all")
        arrive(buf, index)
        got = summed(buf)
        return got[:, :total], got[:, total:total + 1]

    def rows_part(lifted):
        expanded = jnp.sum(tri_row[...] * lifted, axis=1, keepdims=True)
        return jnp.sum(ktile[...] * expanded, axis=0, keepdims=True)

    lifted, norm_now = condition(rh, vec_buf.at[0], 2)
    kept = jnp.zeros((1, rb), jnp.float32)
    for turn in range(ITERS - 1):
        base = 3 + 3 * turn
        rows_buf = row_buf.at[turn]
        rows_buf[c] = rows_part(lifted)
        publish(rows_buf, c, base, "cent")
        arrive(rows_buf, base)
        rows = summed(rows_buf)
        columns = jnp.sum(ktile[...] * rows, axis=1, keepdims=True)
        buf = vec_buf.at[1 + 2 * turn]
        buf[me, :, :total] = jnp.sum(tri_row[...] * columns, axis=0, keepdims=True)
        buf[me, :, total:] = tail(square(rows) / n_c)
        publish(buf, me, base + 1, "all")
        arrive(buf, base + 1)
        got = summed(buf)
        mapped = got[:, :total] / total_rows + ridge_weight * lifted
        energy = got[:, total:total + 1] / total_rows + ridge_weight * square(lifted)
        step_size = norm_now / energy
        kept = kept + step_size * rows
        rh = rh - step_size * mapped
        fresh, norm_next = condition(rh, vec_buf.at[2 + 2 * turn], base + 2)
        lifted = fresh + (norm_next / norm_now) * lifted
        norm_now = norm_next

    last = 3 * ITERS
    all_buf[me] = rows_part(lifted)
    publish(all_buf, me, last, "all")
    arrive(all_buf, last)
    if n_s <= 8:
        energy = jnp.zeros((1, 1), jnp.float32)
        for k in range(n_s):
            energy = energy + square(summed(all_buf, k * n_c, n_c))
    else:
        energy = lax.fori_loop(
            0, n_s, lambda k, acc: acc + square(summed(all_buf, k * n_c, n_c)), jnp.zeros((1, 1), jnp.float32))
    rows = summed(all_buf, s * n_c, n_c)
    step_size = norm_now / (energy / total_rows + ridge_weight * square(lifted))
    fitted[...] = kept + step_size * rows

    pltpu.make_async_copy(moved, moved, tri_sem.at[1]).wait()
    if split:
        chain_finish()
        settle(col_buf, 0)
    settle(rhs_buf, 1)
    settle(vec_buf.at[0], 2)
    for turn in range(ITERS - 1):
        base = 3 + 3 * turn
        settle(row_buf.at[turn], base)
        settle(vec_buf.at[1 + 2 * turn], base + 1)
        settle(vec_buf.at[2 + 2 * turn], base + 2)
    settle(all_buf, last)


def body(samples, targets, centres, tri_inv, inner_inv):
    n_s, n_c = lax.axis_size("samp"), lax.axis_size("cent")
    n = n_s * n_c
    rb, feat = samples.shape
    cb = centres.shape[0]
    sb = tri_inv.shape[1]
    total = sb * n_s
    split = sb % LANES == 0
    if split:
        tri, inner = tri_inv, inner_inv
    else:
        tri, inner = lax.all_gather(tri_inv, "samp", axis=1, tiled=True), inner_inv.T
    chunks = rb // min(256, rb)
    wide = total + LANES
    f32 = jnp.float32
    vmem = pl.BlockSpec(memory_space=pltpu.VMEM)
    hbm = pl.BlockSpec(memory_space=pl.ANY)
    out = pl.pallas_call(
        functools.partial(kernel, n_s, n_c, split),
        out_shape=jax.ShapeDtypeStruct((1, rb), f32),
        in_specs=[hbm, vmem, vmem, hbm, vmem],
        out_specs=vmem,
        scratch_shapes=[
            pltpu.VMEM((rb, feat), samples.dtype),
            pltpu.VMEM((cb, rb), f32),
            pltpu.VMEM((cb, total), f32),
            pltpu.VMEM((sb, cb), f32),
            pltpu.VMEM((sb // n_c, total), f32),
            pltpu.VMEM((n_s, 1, cb), f32),
            pltpu.VMEM((n, 1, sb if split else total), f32),
            pltpu.VMEM((2 * ITERS - 1, n, 1, wide), f32),
            pltpu.VMEM((ITERS - 1, n_c, 1, rb), f32),
            pltpu.VMEM((n, 1, rb), f32),
            pltpu.SemaphoreType.DMA((chunks,)),
            pltpu.SemaphoreType.DMA((4,)),
            pltpu.SemaphoreType.DMA((2, n_s)),
            pltpu.SemaphoreType.DMA((2, n_s)),
            pltpu.SemaphoreType.DMA((3 * ITERS + 1,)),
            pltpu.SemaphoreType.DMA((3 * ITERS + 1,)),
        ],
        compiler_params=pltpu.CompilerParams(
            collective_id=0, has_side_effects=True, vmem_limit_bytes=48 * 2 ** 20),
    )(samples, targets.reshape(1, rb), centres, tri, inner)
    return out.reshape(rb)


def solution(mesh):
    in_specs = (
        P(("groups", "samp"), None),
        P(("groups", "samp")),
        P(("groups", "cent"), None),
        P(("groups", "cent"), "samp"),
        P(("groups", "cent"), "samp"),
    )
    out_specs = P(("groups", "samp"))
    return jax.shard_map(body, mesh=mesh, in_specs=in_specs, out_specs=out_specs, check_vma=False)
```

time: 238 us -> 54.7 us (0.23)
  blocking collectives: 140 us -> 0 us
  Pallas kernels: 0 us -> 48.6 us
  matrix products: 35.8 us -> 0 us
  waiting for transfers between devices: 34.4 us -> 0 us
  between operations: 18 us -> 0.01 us
  other arithmetic: 5.04 us -> 0 us
  local copies, waits for them, and re-layouts: 3.35 us -> 5.81 us
    psum x9 -> x0, blocking collectives: 72.2 us -> none  [the longest x3 32.6 us: kernel_back(): return lax.psum(apply_cols(vector), 'samp')]
    pallas_call x0 -> x1, Pallas kernels: none -> 48.6 us  [body(): pl.pallas_call(functools.partial(kernel, n_s, n_c, split), out_shape=jax....]
    unnamed x6 -> x0, blocking collectives: 36.9 us -> none
    dot_general x36 -> x0, matrix products: 35.8 us -> none  [the longest x12 18.1 us: kernel_tile(): lax.dot_general(sample_block, centres, (((1,), (1,)), ((), ())), preferre...]
    all_gather x2 -> x0, waiting for transfers between devices: 33 us -> none  [the longest x1 20.7 us: body(): lax.all_gather(inner_inv, 'samp', axis=1, tiled=True)]
    all_gather x6 -> x0, blocking collectives: 30.4 us -> none  [forward(): joined = lax.all_gather(vector, 'cent', axis=0, tiled=True)]
    unnamed x18 -> x11, local copies, waits for them, and re-layouts: 0.73 us -> 5.81 us
  transfers between devices with their start and end apart: 2 -> 0, of which waited for: 2 -> 0; matrix products, arithmetic and copies ran while one was open for 3% -> 0% of each run, Pallas kernels for 0% -> 0%
where the time goes in v1:
time: 54.7 us; the launch traced here: 54.4 us
  Pallas kernels  48.6 us (89%)
  local copies, waits for them, and re-layouts  5.81 us (11%)
    pallas_call x1, Pallas kernels, body(): pl.pallas_call(functools.partial(kernel, n_s, n_c, split), out_shape=jax....  48.6 us
    unnamed x11, local copies, waits for them, and re-layouts  5.81 us

profile of v1, /device:TPU:0, one launch (start us, length us, event | category | flops | bytes accessed | tf_op | source)
XLA Modules:
  0.0 54.4 jit_solution(16547372294527957721)
XLA Ops:
  0.0 0.0 copy-start
  0.0 1.6 %copy-done = bf16[1024,1024]{1,0:T(8,128)(2,1)S(1)} copy-done((bf16[1024,1024]{1,0:T(8,128)(2,1)S(1)}, bf16[1024,1024]{1,0:T(8,128)(2,1)}, u32[]{:S(2)}) %copy-start) | copy-done | bytes 2097176
  1.6 0.0 copy-start.1
  1.6 1.0 %copy-done.1 = bf16[256,1024]{1,0:T(8,128)(2,1)S(1)} copy-done((bf16[256,1024]{1,0:T(8,128)(2,1)S(1)}, bf16[256,1024]{1,0:T(8,128)(2,1)}, u32[]{:S(2)}) %copy-start.1) | copy-done | bytes 524312
  2.6 0.0 copy-start.2
  2.6 0.9 %copy-done.2 = f32[256,256]{1,0:T(8,128)S(1)} copy-done((f32[256,256]{1,0:T(8,128)S(1)}, f32[256,256]{1,0:T(8,128)}, u32[]{:S(2)}) %copy-start.2) | copy-done | bytes 262168
  3.6 0.0 copy-start.3
  3.6 0.9 %copy-done.3 = f32[256,256]{1,0:T(8,128)S(1)} copy-done((f32[256,256]{1,0:T(8,128)S(1)}, f32[256,256]{1,0:T(8,128)}, u32[]{:S(2)}) %copy-start.3) | copy-done | bytes 262168
  4.5 0.0 copy-start.4
  4.5 0.7 %copy-done.4 = f32[1024]{0:T(1024)S(1)} copy-done((f32[1024]{0:T(1024)S(1)}, f32[1024]{0:T(1024)}, u32[]{:S(2)}) %copy-start.4) | copy-done | bytes 4120
  5.2 48.6 %shard_map.55 = f32[1,1024]{1,0:T(1,128)S(1)} custom-call(bf16[1024,1024]{1,0:T(8,128)(2,1)S(1)} %copy-done, f32[1,1024]{1,0:T(1,128)S(1)} %bitcast.3, bf16[256,1024]{1,0:T(8,128)(2,1)S(1)} %copy-done.1, f32[256,256]{1,0:T(8,128)S(1)} %copy-done.2, f32[256,256]{1,0:T(8,128)S(1)} %copy-done.3), custom_call_target="tpu_custom_call" | custom-call | tf_op jit(solution)/shard_map/pallas_call | solution.py:312
  53.8 0.6 %copy.7 = f32[1024]{0:T(1024)} copy(f32[1024]{0:T(1024)S(1)} %bitcast.2) | data formatting | bytes 8192
Async XLA Ops:
  0.0 1.6 %copy-start = (bf16[1024,1024]{1,0:T(8,128)(2,1)S(1)}, bf16[1024,1024]{1,0:T(8,128)(2,1)}, u32[]{:S(2)}) copy-start(bf16[1024,1024]{1,0:T(8,128)(2,1)} %samples_hbm.1) | copy-start | bytes 6291460
  1.6 1.0 %copy-start.1 = (bf16[256,1024]{1,0:T(8,128)(2,1)S(1)}, bf16[256,1024]{1,0:T(8,128)(2,1)}, u32[]{:S(2)}) copy-start(bf16[256,1024]{1,0:T(8,128)(2,1)} %centres.1) | copy-start | bytes 1572868
  2.6 0.9 %copy-start.2 = (f32[256,256]{1,0:T(8,128)S(1)}, f32[256,256]{1,0:T(8,128)}, u32[]{:S(2)}) copy-start(f32[256,256]{1,0:T(8,128)} %tri.1) | copy-start | bytes 786436
  3.6 0.9 %copy-start.3 = (f32[256,256]{1,0:T(8,128)S(1)}, f32[256,256]{1,0:T(8,128)}, u32[]{:S(2)}) copy-start(f32[256,256]{1,0:T(8,128)} %inner.1) | copy-start | bytes 786436
  4.5 0.7 %copy-start.4 = (f32[1024]{0:T(1024)S(1)}, f32[1024]{0:T(1024)}, u32[]{:S(2)}) copy-start(f32[1024]{0:T(1024)} %param.6) | copy-start | bytes 12292

commit v2 on v1

--- a/solution.py
+++ b/solution.py
@@ -8,6 +8,9 @@
 
 ITERS = 2
 ridge_weight = 0.01
+FIRST_BACK_JOINED = True
+LAST_JOINED = True
+JOINED = FIRST_BACK_JOINED or LAST_JOINED
 MESH = pl.DeviceIdType.MESH
 LANES = 128
 
@@ -26,9 +29,9 @@
     return jnp.sum(jnp.where(r == c, col, 0.0), axis=0, keepdims=True)
 
 
-def kernel(n_s, n_c, split, samples_hbm, targets, centres, tri, inner, fitted,
-           samples, ktile, tri_row, inner_t, joined,
-           col_buf, rhs_buf, vec_buf, row_buf, all_buf,
+def kernel(n_s, n_c, split, samples_hbm, targets_hbm, centres_hbm, tri, inner_hbm, fitted,
+           samples, targets, centres, inner, ktile, tri_row, inner_t, joined,
+           lifted_ref, col_buf, rhs_buf, vec_buf, row_buf, all_buf,
            load_sem, tri_sem, chain_send, chain_recv, send_sem, recv_sem):
     g = lax.axis_index("groups")
     s = lax.axis_index("samp")
@@ -68,8 +71,15 @@
 
     barrier = pltpu.get_barrier_semaphore()
     peers("all", lambda a, b: pl.semaphore_signal(barrier, inc=1, device_id=at(a, b), device_id_type=MESH))
+    load_inner = pltpu.make_async_copy(inner_hbm, inner, load_sem.at[chunks])
+    load_centres = pltpu.make_async_copy(centres_hbm, centres, load_sem.at[chunks + 1])
+    load_targets = pltpu.make_async_copy(targets_hbm, targets, load_sem.at[chunks + 2])
+    load_centres.start()
     for j in range(chunks):
         loads(j).start()
+        if j == 0:
+            load_inner.start()
+    load_targets.start()
 
     def live(k):
         return (k + 1) * sb > c * cb
@@ -83,6 +93,7 @@
     if split:
         own_tri = pltpu.make_async_copy(tri, tri_block(s), tri_sem.at[0])
         own_tri.start()
+        load_inner.wait()
         inner_t[...] = inner[...].T
         for k in range(n_s):
             @pl.when(jnp.logical_not(live(k)) & (k != s))
@@ -91,8 +102,10 @@
     else:
         own_tri = pltpu.make_async_copy(tri, tri_row, tri_sem.at[0])
         own_tri.start()
+        load_inner.wait()
         inner_t[...] = inner[...]
 
+    load_centres.wait()
     centre_vals = centres[...]
     wide = centre_vals.astype(jnp.float32)
     centre_norms = jnp.sum(wide * wide, axis=1, keepdims=True)
@@ -177,7 +190,7 @@
         tile(j)
     pl.semaphore_wait(barrier, n - 1)
     own_tri.wait()
-    if split:
+    if split and JOINED:
         chain_start(0)
 
     def inner_copy(i):
@@ -195,67 +208,105 @@
     for j in range(half, chunks):
         tile(j)
 
+    load_targets.wait()
     aimed = jnp.sum(ktile[...] * targets[...], axis=1, keepdims=True)
-    if split:
-        col_buf[s] = col_to_row(aimed)
-        publish(col_buf, s, 0, "samp")
-        if n_s > 1:
-            chain_wait(1)
-            if n_s > 2:
-                chain_start(1)
-        arrive(col_buf, 0)
-        pulled = row_to_col(summed(col_buf))
-        own_block = tri_row[:, pl.ds(pl.multiple_of(s * sb, LANES), sb)]
-        rhs_buf[me] = jnp.sum(own_block * pulled, axis=0, keepdims=True)
-        publish(rhs_buf, me, 1, "all")
-        for j in range(2, n_s):
+
+    def over_samp(col, slot, index, between=None):
+        buf = col_buf.at[slot]
+        buf[s] = col_to_row(col)
+        publish(buf, s, index, "samp")
+        if between is not None:
+            between()
+        arrive(buf, index)
+        return row_to_col(summed(buf))
+
+    def own_block():
+        return tri_row[:, pl.ds(pl.multiple_of(s * sb, LANES), sb)]
+
+    def pull_blocks(col, scalar, slot, index, between=None):
+        buf = rhs_buf.at[slot]
+        buf[me, :, :sb] = jnp.sum(own_block() * col, axis=0, keepdims=True)
+        buf[me, :, sb:] = tail(scalar)
+        publish(buf, me, index, "all")
+        if between is not None:
+            between()
+        arrive(buf, index)
+        blocks = [summed(buf, k * n_c, n_c) for k in range(n_s)]
+        scalar = blocks[0][:, sb:sb + 1]
+        for k in range(1, n_s):
+            scalar = scalar + blocks[k][:, sb:sb + 1]
+        return jnp.concatenate([block[:, :sb] for block in blocks], axis=1), scalar
+
+    def chain_step(j):
+        if split and JOINED and 0 < j < n_s:
             chain_wait(j)
             if j < n_s - 1:
                 chain_start(j)
-        arrive(rhs_buf, 1)
-        rh = jnp.concatenate([summed(rhs_buf, k * n_c, n_c) for k in range(n_s)], axis=1)
+
+    extra = 3 * ITERS + 1
+    zero = jnp.zeros((1, 1), jnp.float32)
+    if split:
+        pulled = over_samp(aimed, 0, 0)
+        rh, _ = pull_blocks(pulled, zero, 0, 1, lambda: chain_step(1))
     else:
-        rhs_buf[me] = jnp.sum(tri_row[...] * aimed, axis=0, keepdims=True)
-        publish(rhs_buf, me, 1, "all")
-        arrive(rhs_buf, 1)
-        rh = summed(rhs_buf)
+        buf = rhs_buf.at[0]
+        buf[me] = jnp.sum(tri_row[...] * aimed, axis=0, keepdims=True)
+        publish(buf, me, 1, "all")
+        arrive(buf, 1)
+        rh = summed(buf)
     rh = rh / total_rows
 
     moved = inner_t.at[pl.ds(0, (n_c - 1) * part)]
     pltpu.make_async_copy(moved, moved, tri_sem.at[2]).wait()
     own_inner.wait()
 
-    def condition(vector, buf, index):
+    def condition(vector, buf, index, between=None):
         picked = jnp.sum(joined[...] * vector, axis=1, keepdims=True)
         buf[me, :, :total] = jnp.sum(joined[...] * picked, axis=0, keepdims=True)
         buf[me, :, total:] = tail(jnp.sum(picked * picked, axis=0, keepdims=True))
         publish(buf, me, index, "all")
+        if between is not None:
+            between()
         arrive(buf, index)
         got = summed(buf)
         return got[:, :total], got[:, total:total + 1]
 
-    def rows_part(lifted):
-        expanded = jnp.sum(tri_row[...] * lifted, axis=1, keepdims=True)
+    def rows_part(lifted, joined_rows, slot, index, between=None):
+        if joined_rows:
+            expanded = jnp.sum(tri_row[...] * lifted, axis=1, keepdims=True)
+        else:
+            lifted_ref[...] = lifted
+            mine = lifted_ref[:, pl.ds(pl.multiple_of(s * sb, LANES), sb)]
+            expanded = over_samp(jnp.sum(own_block() * mine, axis=1, keepdims=True), slot, index, between)
         return jnp.sum(ktile[...] * expanded, axis=0, keepdims=True)
 
-    lifted, norm_now = condition(rh, vec_buf.at[0], 2)
+    lifted, norm_now = condition(rh, vec_buf.at[0], 2, lambda: chain_step(2))
     kept = jnp.zeros((1, rb), jnp.float32)
     for turn in range(ITERS - 1):
         base = 3 + 3 * turn
         rows_buf = row_buf.at[turn]
-        rows_buf[c] = rows_part(lifted)
+        first = split and turn == 0
+        rows_buf[c] = rows_part(lifted, not first, 1, extra)
         publish(rows_buf, c, base, "cent")
         arrive(rows_buf, base)
         rows = summed(rows_buf)
         columns = jnp.sum(ktile[...] * rows, axis=1, keepdims=True)
-        buf = vec_buf.at[1 + 2 * turn]
-        buf[me, :, :total] = jnp.sum(tri_row[...] * columns, axis=0, keepdims=True)
-        buf[me, :, total:] = tail(square(rows) / n_c)
-        publish(buf, me, base + 1, "all")
-        arrive(buf, base + 1)
-        got = summed(buf)
-        mapped = got[:, :total] / total_rows + ridge_weight * lifted
-        energy = got[:, total:total + 1] / total_rows + ridge_weight * square(lifted)
+        if first:
+            for j in range(3, n_s):
+                chain_step(j)
+        if first and not FIRST_BACK_JOINED:
+            columns = over_samp(columns, 2, extra + 1)
+            back, scalar = pull_blocks(columns, square(rows) / n_c, 1, base + 1)
+        else:
+            buf = vec_buf.at[1 + 2 * turn]
+            buf[me, :, :total] = jnp.sum(tri_row[...] * columns, axis=0, keepdims=True)
+            buf[me, :, total:] = tail(square(rows) / n_c)
+            publish(buf, me, base + 1, "all")
+            arrive(buf, base + 1)
+            got = summed(buf)
+            back, scalar = got[:, :total], got[:, total:total + 1]
+        mapped = back / total_rows + ridge_weight * lifted
+        energy = scalar / total_rows + ridge_weight * square(lifted)
         step_size = norm_now / energy
         kept = kept + step_size * rows
         rh = rh - step_size * mapped
@@ -264,7 +315,7 @@
         norm_now = norm_next
 
     last = 3 * ITERS
-    all_buf[me] = rows_part(lifted)
+    all_buf[me] = rows_part(lifted, not split or LAST_JOINED, 3, extra + 2)
     publish(all_buf, me, last, "all")
     arrive(all_buf, last)
     if n_s <= 8:
@@ -280,14 +331,23 @@
 
     pltpu.make_async_copy(moved, moved, tri_sem.at[1]).wait()
     if split:
-        chain_finish()
-        settle(col_buf, 0)
-    settle(rhs_buf, 1)
+        if JOINED:
+            chain_finish()
+        settle(col_buf.at[0], 0)
+        settle(col_buf.at[1], extra)
+        if not FIRST_BACK_JOINED:
+            settle(col_buf.at[2], extra + 1)
+        if not LAST_JOINED:
+            settle(col_buf.at[3], extra + 2)
+    settle(rhs_buf.at[0], 1)
     settle(vec_buf.at[0], 2)
     for turn in range(ITERS - 1):
         base = 3 + 3 * turn
         settle(row_buf.at[turn], base)
-        settle(vec_buf.at[1 + 2 * turn], base + 1)
+        if split and turn == 0 and not FIRST_BACK_JOINED:
+            settle(rhs_buf.at[1], base + 1)
+        else:
+            settle(vec_buf.at[1 + 2 * turn], base + 1)
         settle(vec_buf.at[2 + 2 * turn], base + 2)
     settle(all_buf, last)
 
@@ -308,32 +368,36 @@
     wide = total + LANES
     f32 = jnp.float32
     vmem = pl.BlockSpec(memory_space=pltpu.VMEM)
-    hbm = pl.BlockSpec(memory_space=pl.ANY)
+    hbm = pl.BlockSpec(memory_space=pltpu.HBM)
     out = pl.pallas_call(
         functools.partial(kernel, n_s, n_c, split),
         out_shape=jax.ShapeDtypeStruct((1, rb), f32),
-        in_specs=[hbm, vmem, vmem, hbm, vmem],
+        in_specs=[hbm] * 5,
         out_specs=vmem,
         scratch_shapes=[
             pltpu.VMEM((rb, feat), samples.dtype),
+            pltpu.VMEM((1, rb), f32),
+            pltpu.VMEM((cb, feat), centres.dtype),
+            pltpu.VMEM(inner.shape, f32),
             pltpu.VMEM((cb, rb), f32),
             pltpu.VMEM((cb, total), f32),
             pltpu.VMEM((sb, cb), f32),
             pltpu.VMEM((sb // n_c, total), f32),
-            pltpu.VMEM((n_s, 1, cb), f32),
-            pltpu.VMEM((n, 1, sb if split else total), f32),
+            pltpu.VMEM((1, total), f32),
+            pltpu.VMEM((4, n_s, 1, cb), f32),
+            pltpu.VMEM((2, n, 1, sb + LANES if split else total), f32),
             pltpu.VMEM((2 * ITERS - 1, n, 1, wide), f32),
             pltpu.VMEM((ITERS - 1, n_c, 1, rb), f32),
             pltpu.VMEM((n, 1, rb), f32),
-            pltpu.SemaphoreType.DMA((chunks,)),
+            pltpu.SemaphoreType.DMA((chunks + 3,)),
             pltpu.SemaphoreType.DMA((4,)),
             pltpu.SemaphoreType.DMA((2, n_s)),
             pltpu.SemaphoreType.DMA((2, n_s)),
-            pltpu.SemaphoreType.DMA((3 * ITERS + 1,)),
-            pltpu.SemaphoreType.DMA((3 * ITERS + 1,)),
+            pltpu.SemaphoreType.DMA((3 * ITERS + 4,)),
+            pltpu.SemaphoreType.DMA((3 * ITERS + 4,)),
         ],
         compiler_params=pltpu.CompilerParams(
-            collective_id=0, has_side_effects=True, vmem_limit_bytes=48 * 2 ** 20),
+            collective_id=0, has_side_effects=True, vmem_limit_bytes=60 * 2 ** 20),
     )(samples, targets.reshape(1, rb), centres, tri, inner)
     return out.reshape(rb)
 

time: 54.7 us -> 46.6 us (0.85)
  local copies, waits for them, and re-layouts: 5.81 us -> 1.28 us
  Pallas kernels: 48.6 us -> 45.1 us
    unnamed x11 -> x1, local copies, waits for them, and re-layouts: 5.81 us -> 1.28 us
    pallas_call x1, Pallas kernels: 48.6 us -> 45.1 us  [body(): pl.pallas_call(functools.partial(kernel, n_s, n_c, split), out_shape=jax....]
where the time goes in v2:
time: 46.6 us; the launch traced here: 46.4 us
  Pallas kernels  45.1 us (97%)
  local copies, waits for them, and re-layouts  1.28 us (3%)
    pallas_call x1, Pallas kernels, body(): pl.pallas_call(functools.partial(kernel, n_s, n_c, split), out_shape=jax....  45.1 us
    unnamed x1, local copies, waits for them, and re-layouts  1.28 us

profile of v2, /device:TPU:0, one launch (start us, length us, event | category | flops | bytes accessed | tf_op | source)
XLA Modules:
  0.0 46.4 jit_solution(7213297556010950339)
XLA Ops:
  0.0 45.1 %shard_map.55 = f32[1,1024]{1,0:T(1,128)} custom-call(bf16[1024,1024]{1,0:T(8,128)(2,1)} %samples_hbm.1, f32[1,1024]{1,0:T(1,128)} %bitcast.3, bf16[256,1024]{1,0:T(8,128)(2,1)} %centres_hbm.1, f32[256,256]{1,0:T(8,128)} %tri.1, f32[256,256]{1,0:T(8,128)} %inner_hbm.1), custom_call_target="tpu_custom_call" | custom-call | tf_op jit(solution)/shard_map/pallas_call | solution.py:372
  45.1 1.3 %copy.7 = f32[1024]{0:T(1024)} copy(f32[1024]{0:T(1024)} %bitcast.2) | data formatting | bytes 8192

commit v3 on v2

--- a/solution.py
+++ b/solution.py
@@ -10,6 +10,7 @@
 ridge_weight = 0.01
 FIRST_BACK_JOINED = True
 LAST_JOINED = True
+PIECES = 1
 JOINED = FIRST_BACK_JOINED or LAST_JOINED
 MESH = pl.DeviceIdType.MESH
 LANES = 128
@@ -50,20 +51,26 @@
     def at(ss, cc):
         return {"groups": g, "samp": ss, "cent": cc}
 
-    def each(count, act):
+    def each(count, order, act):
         if count <= 16:
-            for i in range(1, count):
+            for i in order:
                 act(i)
         else:
             lax.fori_loop(1, count, lambda i, z: (act(i), z)[1], 0)
 
+    def reach(i):
+        a, b = i // n_c, i % n_c
+        return (max(a, n_s - a) if a else 0) + (1 if b > 1 else 0)
+
+    far_first = sorted(range(1, n), key=lambda i: -reach(i))
+
     def peers(kind, act):
         if kind == "samp":
-            each(n_s, lambda i: act(lax.rem(s + i, n_s), c))
+            each(n_s, sorted(range(1, n_s), key=lambda i: -max(i, n_s - i)), lambda i: act(lax.rem(s + i, n_s), c))
         elif kind == "cent":
-            each(n_c, lambda i: act(s, lax.rem(c + i, n_c)))
+            each(n_c, range(1, n_c), lambda i: act(s, lax.rem(c + i, n_c)))
         else:
-            each(n, lambda i: act(lax.rem(s + i // n_c, n_s), lax.rem(c + i % n_c, n_c)))
+            each(n, far_first, lambda i: act(lax.rem(s + i // n_c, n_s), lax.rem(c + i % n_c, n_c)))
 
     def loads(j):
         rows = pl.ds(j * chunk, chunk)
@@ -119,11 +126,15 @@
                                   preferred_element_type=jnp.float32)
         ktile[:, j * chunk:(j + 1) * chunk] = jnp.exp((2.0 * crossed - norms - centre_norms) * (1.0 / feat))
 
-    def hop(way, j):
+    def hop(way, j, piece=None):
         k = s - way * j
         lane = (1 - way) // 2
+        where = tri_block(k)
+        if piece is not None:
+            rows = cb // PIECES
+            where = tri_row.at[pl.ds(piece * rows, rows), pl.ds(pl.multiple_of(k * sb, LANES), sb)]
         return pltpu.make_async_remote_copy(
-            src_ref=tri_block(k), dst_ref=tri_block(k),
+            src_ref=where, dst_ref=where,
             send_sem=chain_send.at[lane, j], recv_sem=chain_recv.at[lane, j],
             device_id=at(s + way, c), device_id_type=MESH)
 
@@ -131,12 +142,13 @@
         return (k >= 0) & (k < n_s)
 
     def chain_start(j):
-        for way in (1, -1):
+        for way in (-1, 1):
             k = s - way * j
 
             @pl.when(inside(k) & inside(s + way) & live(k))
             def _():
-                hop(way, j).start()
+                for piece in range(PIECES):
+                    hop(way, j, piece).start()
 
     def chain_wait(j):
         for way in (1, -1):
@@ -280,13 +292,13 @@
             expanded = over_samp(jnp.sum(own_block() * mine, axis=1, keepdims=True), slot, index, between)
         return jnp.sum(ktile[...] * expanded, axis=0, keepdims=True)
 
-    lifted, norm_now = condition(rh, vec_buf.at[0], 2, lambda: chain_step(2))
+    lifted, norm_now = condition(rh, vec_buf.at[0], 2)
     kept = jnp.zeros((1, rb), jnp.float32)
     for turn in range(ITERS - 1):
         base = 3 + 3 * turn
         rows_buf = row_buf.at[turn]
         first = split and turn == 0
-        rows_buf[c] = rows_part(lifted, not first, 1, extra)
+        rows_buf[c] = rows_part(lifted, not first, 1, extra, (lambda: chain_step(2)) if first else None)
         publish(rows_buf, c, base, "cent")
         arrive(rows_buf, base)
         rows = summed(rows_buf)

time: 46.6 us -> 45 us (0.966)
  Pallas kernels: 45.1 us -> 43.5 us
    pallas_call x1, Pallas kernels: 45.1 us -> 43.5 us  [body(): pl.pallas_call(functools.partial(kernel, n_s, n_c, split), out_shape=jax....]
where the time goes in v3:
time: 45 us; the launch traced here: 44.8 us
  Pallas kernels  43.5 us (97%)
  local copies, waits for them, and re-layouts  1.28 us (3%)
    pallas_call x1, Pallas kernels, body(): pl.pallas_call(functools.partial(kernel, n_s, n_c, split), out_shape=jax....  43.5 us
    unnamed x1, local copies, waits for them, and re-layouts  1.28 us

profile of v3, /device:TPU:0, one launch (start us, length us, event | category | flops | bytes accessed | tf_op | source)
XLA Modules:
  0.0 44.8 jit_solution(3823855208493182914)
XLA Ops:
  0.0 43.5 %shard_map.55 = f32[1,1024]{1,0:T(1,128)} custom-call(bf16[1024,1024]{1,0:T(8,128)(2,1)} %samples_hbm.1, f32[1,1024]{1,0:T(1,128)} %bitcast.3, bf16[256,1024]{1,0:T(8,128)(2,1)} %centres_hbm.1, f32[256,256]{1,0:T(8,128)} %tri.1, f32[256,256]{1,0:T(8,128)} %inner_hbm.1), custom_call_target="tpu_custom_call" | custom-call | tf_op jit(solution)/shard_map/pallas_call | solution.py:384
  43.5 1.3 %copy.7 = f32[1024]{0:T(1024)} copy(f32[1024]{0:T(1024)} %bitcast.2) | data formatting | bytes 8192

commit v4 on v3

--- a/solution.py
+++ b/solution.py
@@ -197,7 +197,7 @@
     def square(vector):
         return jnp.sum(vector * vector, axis=1, keepdims=True)
 
-    half = chunks // 2
+    half = 0
     for j in range(half):
         tile(j)
     pl.semaphore_wait(barrier, n - 1)

time: 45 us -> 44.9 us (level)
  no operation moved by 1% of the time
where the time goes in v4:
time: 44.9 us; the launch traced here: 44.7 us
  Pallas kernels  43.4 us (97%)
  local copies, waits for them, and re-layouts  1.28 us (3%)
    pallas_call x1, Pallas kernels, body(): pl.pallas_call(functools.partial(kernel, n_s, n_c, split), out_shape=jax....  43.4 us
    unnamed x1, local copies, waits for them, and re-layouts  1.28 us

profile of v4, /device:TPU:0, one launch (start us, length us, event | category | flops | bytes accessed | tf_op | source)
XLA Modules:
  0.0 44.7 jit_solution(12101331945940142589)
XLA Ops:
  0.0 43.4 %shard_map.55 = f32[1,1024]{1,0:T(1,128)} custom-call(bf16[1024,1024]{1,0:T(8,128)(2,1)} %samples_hbm.1, f32[1,1024]{1,0:T(1,128)} %bitcast.3, bf16[256,1024]{1,0:T(8,128)(2,1)} %centres_hbm.1, f32[256,256]{1,0:T(8,128)} %tri.1, f32[256,256]{1,0:T(8,128)} %inner_hbm.1), custom_call_target="tpu_custom_call" | custom-call | tf_op jit(solution)/shard_map/pallas_call | solution.py:384
  43.4 1.3 %copy.7 = f32[1024]{0:T(1024)} copy(f32[1024]{0:T(1024)} %bitcast.2) | data formatting | bytes 8192
